TPU v7x, 256 devices: a whole 4x4x8 slice. The times are simulated.
256 devices in a mesh: snap: 16 (over z, core), vtx: 16 (over y, x).
Axes of the slice: x: 4, y: 4, z: 8, core: 2. Of those that a mesh axis runs over, the one named last changes fastest.
Arguments:
- feats: float32 [16, 16384, 512], P('snap', 'vtx'), may hold values from -6 to 6
- col_ids: int32 [16, 128, 16], P('snap', 'vtx'), may hold values from 0 to 127
- tiles: float32 [16, 128, 16, 128, 128], P('snap', 'vtx'), may hold values from -0.125 to 0.125
- w_first: float32 [512, 256], replicated, may hold values from -0.25 to 0.25
- w_input: float32 [256, 1024], replicated, may hold values from -0.375 to 0.375
- w_recur: float32 [256, 1024], replicated, may hold values from -0.375 to 0.375
- lstm_bias: float32 [1024], replicated, may hold values from -3 to 3
- w_second: float32 [256, 256], replicated, may hold values from -0.375 to 0.375
Outputs:
- output: float32 [16, 16384, 256], P('snap', 'vtx')
Inputs may be any that keep to these rules, and one draw needn't show every extreme that they name: `col_ids`: every entry names a row block of the same snapshot's graph; a few blocks are named far more often than others.
All inputs are finite; a program needn't handle non-finite values.
Results may differ from a plain program's by a relative error of at most 0.0003.
Values sent between devices are 32-bit elements; how exact they have to be, the bound alone decides.
A program may use at most 128 MiB of HBM per device.

v0:
```python
import jax
import jax.numpy as jnp
from jax import lax
from jax.sharding import PartitionSpec as P


def block_sum(tile_set, column_ids, source):
    tile_edge = tile_set.shape[-1]
    width = source.shape[-1]
    blocks = source.reshape(source.shape[0] // tile_edge, tile_edge, width)

    def row_block(operands):
        tiles_here, ids_here = operands
        picked = blocks[ids_here]
        return jnp.einsum("ktu,kuw->tw", tiles_here, picked, precision=lax.Precision.HIGHEST)

    summed = lax.map(row_block, (tile_set, column_ids))
    return summed.reshape(-1, width)


def row_scale(tiles):
    sums = jnp.sum(tiles * tiles, axis=(2, 4))
    return lax.rsqrt(1.0 + sums).reshape(tiles.shape[0], -1)[..., None]


def recurrence(pre_time, w_recur, lstm_bias):
    hidden_size = w_recur.shape[0]

    def advance(carry, pre_step):
        state_h, state_c = carry
        gates = pre_step + jnp.dot(state_h, w_recur, precision=lax.Precision.HIGHEST) + lstm_bias
        gate_i = gates[:, :hidden_size]
        gate_f = gates[:, hidden_size : 2 * hidden_size]
        gate_g = gates[:, 2 * hidden_size : 3 * hidden_size]
        gate_o = gates[:, 3 * hidden_size :]
        state_c = jax.nn.sigmoid(gate_f) * state_c + jax.nn.sigmoid(gate_i) * jnp.tanh(gate_g)
        state_h = jax.nn.sigmoid(gate_o) * jnp.tanh(state_c)
        return ((state_h, state_c), state_h)

    zeros = jnp.zeros((pre_time.shape[1], hidden_size), jnp.float32)
    _, states = lax.scan(advance, (zeros, zeros), pre_time)
    return states


def on_device(feats, col_ids, tiles, w_first, w_input, w_recur, lstm_bias, w_second):
    scale = row_scale(tiles)
    whole = lax.all_gather(feats, "vtx", axis=1, tiled=True)
    mixed = scale * (feats + jax.vmap(block_sum)(tiles, col_ids, whole))
    hidden_one = jax.nn.relu(
        jnp.einsum("svf,fh->svh", mixed, w_first, precision=lax.Precision.HIGHEST)
    )
    timelines = lax.all_to_all(hidden_one, "snap", split_axis=1, concat_axis=0, tiled=True)
    pre_time = jnp.einsum("svh,hg->svg", timelines, w_input, precision=lax.Precision.HIGHEST)
    states = recurrence(pre_time, w_recur, lstm_bias)
    returned = lax.all_to_all(states, "snap", split_axis=0, concat_axis=1, tiled=True)
    whole_two = lax.all_gather(returned, "vtx", axis=1, tiled=True)
    mixed_two = scale * (returned + jax.vmap(block_sum)(tiles, col_ids, whole_two))
    return jnp.einsum("svh,hg->svg", mixed_two, w_second, precision=lax.Precision.HIGHEST)


def solution(mesh):
    placed = (
        P("snap", "vtx", None),
        P("snap", "vtx", None),
        P("snap", "vtx", None, None, None),
        P(),
        P(),
        P(),
        P(),
        P(),
    )
    return jax.shard_map(
        on_device, mesh=mesh, in_specs=placed, out_specs=P("snap", "vtx", None), check_vma=False
    )
```

profile of v0, /device:TPU:1, one launch (start us, length us, event | category | flops | bytes accessed | tf_op | source)
XLA Modules:
  0.0 617.5 jit_solution(13330983946178340313)
XLA Ops:
  11.3 204.4 %all-gather.3.cloned.1.call-done = f32[1,16384,512]{2,1,0:T(8,128)} async-done(((f32[1,1024,512]{2,1,0:T(8,128)}), f32[1,16384,512]{2,1,0:T(8,128)}) %all-gather.3.cloned.1.call-update) | async-done | bytes 33554448 | tf_op jit(solution)/shard_map/all_gather | solution.py:47
  215.7 91.2 %while.35 = (s32[]{:T(128)}, f32[8,1,128,512]{3,2,1,0:T(8,128)}, f32[8,1,16,128,128]{4,3,2,1,0:T(8,128)}, s32[8,1,16]{2,1,0:T(1,128)}, f32[1,128,128,512]{3,2,1,0:T(8,128)}, /*index=5*/s32[]{:T(128)}) while((s32[]{:T(128)}, f32[8,1,128,512]{3,2,1,0:T(8,128)}, f32[8,1,16,128,128]{4,3,2,1,0:T(8,128)}, s32[8,1,16]{2,1,0:T(1,128)}, ...), condition=%wide.region_2.3_spmd, body=%wide.region_1.2_spmd.sunk | while | flops 1610612864 | bytes 13895369 | solution.py:17
  221.6 5.7 fusion.62
  232.9 5.7 fusion.62
  244.3 5.7 fusion.62
  255.7 5.7 fusion.62
  267.2 5.6 fusion.62
  278.6 5.6 fusion.62
  289.9 5.6 fusion.62
  301.2 5.7 fusion.62
  312.5 7.8 %all-to-all-start = ((f32[1,1024,256]{2,0,1:T(1,128)}), f32[1,1024,256]{2,0,1:T(1,128)S(1)}, u32[]{:S(2)}, u32[]{:S(2)}) async-start(f32[1,1024,256]{2,0,1:T(1,128)} %copy.12), calls=%async_computation | async-start | bytes 2097152 | tf_op jit(solution)/shard_map/all_to_all | solution.py:52
  320.4 27.9 %all-to-all-done = f32[1,1024,256]{2,0,1:T(1,128)S(1)} async-done(((f32[1,1024,256]{2,0,1:T(1,128)}), f32[1,1024,256]{2,0,1:T(1,128)S(1)}, u32[]{:S(2)}, u32[]{:S(2)}) %all-to-all-start) | async-done | bytes 1048608 | tf_op jit(solution)/shard_map/all_to_all | solution.py:52
  353.3 29.0 %while.37 = (s32[]{:T(128)}, f32[64,256]{1,0:T(8,128)S(1)}, f32[64,256]{1,0:T(8,128)S(1)}, f32[16,64,256]{2,1,0:T(8,128)S(1)}, f32[16,64,1024]{2,1,0:T(8,128)}, ...) while((s32[]{:T(128)}, f32[64,256]{1,0:T(8,128)S(1)}, ...), condition=%wide.region_4.5_spmd.clone, body=%wide.region_3.4_spmd.clone.sunk | while | flops 201703424 | bytes 2166896 | solution.py:41
  382.4 32.0 %all_to_all.27 = f32[16,64,256]{2,1,0:T(8,128)} all-to-all(f32[16,64,256]{2,1,0:T(8,128)S(1)} %get-tuple-element.97), channel_id=1, replica_groups=mesh['snap'=16,'vtx'=16] {'snap'}, dimensions={0} | all-to-all | bytes 2097152 | tf_op jit(solution)/shard_map/all_to_all | solution.py:55
  414.4 111.3 %all-gather.5.cloned.1.call-done = f32[1,16384,256]{2,1,0:T(8,128)} async-done(((f32[1,1024,256]{2,1,0:T(8,128)}), f32[1,16384,256]{2,1,0:T(8,128)}) %all-gather.5.cloned.1.call-update) | async-done | bytes 16777232 | tf_op jit(solution)/shard_map/all_gather | solution.py:56
  525.7 81.2 %while.36 = (s32[]{:T(128)}, f32[8,1,128,256]{3,2,1,0:T(8,128)}, f32[8,1,16,128,128]{4,3,2,1,0:T(8,128)}, s32[8,1,16]{2,1,0:T(1,128)}, f32[1,128,128,256]{3,2,1,0:T(8,128)}, /*index=5*/s32[]{:T(128)}) while((s32[]{:T(128)}, f32[8,1,128,256]{3,2,1,0:T(8,128)}, f32[8,1,16,128,128]{4,3,2,1,0:T(8,128)}, s32[8,1,16]{2,1,0:T(1,128)}, ...), condition=%wide.region_6.7_spmd, body=%wide.region_5.6_spmd.sunk | while | flops 805306496 | bytes 7472841 | solution.py:17
  526.4 6.4 %gather_fusion.1 = f32[16,128,256]{2,1,0:T(8,128)S(1)} fusion(f32[1,128,128,256]{3,2,1,0:T(8,128)} %get-tuple-element.352, s32[16]{0:T(128)S(1)} %or_bitcast_fusion.5), kind=kCustom, calls=%fused_computation.1.clone.1 | custom fusion | bytes 4194432 | tf_op jit(solution)/shard_map/vmap()/while/body/eval_jaxpr/gather | solution.py:14
  536.5 6.4 %gather_fusion.1 = f32[16,128,256]{2,1,0:T(8,128)S(1)} fusion(f32[1,128,128,256]{3,2,1,0:T(8,128)} %get-tuple-element.352, s32[16]{0:T(128)S(1)} %or_bitcast_fusion.5), kind=kCustom, calls=%fused_computation.1.clone.1 | custom fusion | bytes 4194432 | tf_op jit(solution)/shard_map/vmap()/while/body/eval_jaxpr/gather | solution.py:14
  546.7 6.4 %gather_fusion.1 = f32[16,128,256]{2,1,0:T(8,128)S(1)} fusion(f32[1,128,128,256]{3,2,1,0:T(8,128)} %get-tuple-element.352, s32[16]{0:T(128)S(1)} %or_bitcast_fusion.5), kind=kCustom, calls=%fused_computation.1.clone.1 | custom fusion | bytes 4194432 | tf_op jit(solution)/shard_map/vmap()/while/body/eval_jaxpr/gather | solution.py:14
  556.8 6.4 %gather_fusion.1 = f32[16,128,256]{2,1,0:T(8,128)S(1)} fusion(f32[1,128,128,256]{3,2,1,0:T(8,128)} %get-tuple-element.352, s32[16]{0:T(128)S(1)} %or_bitcast_fusion.5), kind=kCustom, calls=%fused_computation.1.clone.1 | custom fusion | bytes 4194432 | tf_op jit(solution)/shard_map/vmap()/while/body/eval_jaxpr/gather | solution.py:14
  567.0 6.4 %gather_fusion.1 = f32[16,128,256]{2,1,0:T(8,128)S(1)} fusion(f32[1,128,128,256]{3,2,1,0:T(8,128)} %get-tuple-element.352, s32[16]{0:T(128)S(1)} %or_bitcast_fusion.5), kind=kCustom, calls=%fused_computation.1.clone.1 | custom fusion | bytes 4194432 | tf_op jit(solution)/shard_map/vmap()/while/body/eval_jaxpr/gather | solution.py:14
  577.1 6.4 %gather_fusion.1 = f32[16,128,256]{2,1,0:T(8,128)S(1)} fusion(f32[1,128,128,256]{3,2,1,0:T(8,128)} %get-tuple-element.352, s32[16]{0:T(128)S(1)} %or_bitcast_fusion.5), kind=kCustom, calls=%fused_computation.1.clone.1 | custom fusion | bytes 4194432 | tf_op jit(solution)/shard_map/vmap()/while/body/eval_jaxpr/gather | solution.py:14
  587.3 6.4 %gather_fusion.1 = f32[16,128,256]{2,1,0:T(8,128)S(1)} fusion(f32[1,128,128,256]{3,2,1,0:T(8,128)} %get-tuple-element.352, s32[16]{0:T(128)S(1)} %or_bitcast_fusion.5), kind=kCustom, calls=%fused_computation.1.clone.1 | custom fusion | bytes 4194432 | tf_op jit(solution)/shard_map/vmap()/while/body/eval_jaxpr/gather | solution.py:14
  597.4 6.4 %gather_fusion.1 = f32[16,128,256]{2,1,0:T(8,128)S(1)} fusion(f32[1,128,128,256]{3,2,1,0:T(8,128)} %get-tuple-element.352, s32[16]{0:T(128)S(1)} %or_bitcast_fusion.5), kind=kCustom, calls=%fused_computation.1.clone.1 | custom fusion | bytes 4194432 | tf_op jit(solution)/shard_map/vmap()/while/body/eval_jaxpr/gather | solution.py:14
  (123 shorter events, 123.3 us)
Async XLA Ops:
  6.5 341.8 %copy-start = (f32[256,1024]{1,0:T(8,128)S(1)}, f32[256,1024]{1,0:T(8,128)}, u32[]{:S(2)}) copy-start(f32[256,1024]{1,0:T(8,128)} %param.18) | copy-start | bytes 3145732
  6.5 209.2 %all-gather.3.cloned.1.call-start = ((), (), s32[]{:S(2)}) async-start(), calls=%async_computation.2 | async-start | bytes 35651584 | tf_op jit(solution)/shard_map/all_gather | solution.py:47
  215.7 91.2 %copy-start.2 = (f32[1,1024,512]{2,1,0:T(8,128)S(1)}, f32[1,1024,512]{2,1,0:T(8,128)}, u32[]{:S(2)}) copy-start(f32[1,1024,512]{2,1,0:T(8,128)} %param.14) | copy-start | bytes 6291460
  312.5 35.7 %all-to-all-start = ((f32[1,1024,256]{2,0,1:T(1,128)}), f32[1,1024,256]{2,0,1:T(1,128)S(1)}, u32[]{:S(2)}, u32[]{:S(2)}) async-start(f32[1,1024,256]{2,0,1:T(1,128)} %copy.12), calls=%async_computation | async-start | bytes 2097152 | tf_op jit(solution)/shard_map/all_to_all | solution.py:52
  320.3 205.4 %all-gather.5.cloned.1.call-start = ((), (), s32[]{:S(2)}) async-start(), calls=%async_computation.3 | async-start | bytes 17825792 | tf_op jit(solution)/shard_map/all_gather | solution.py:56
  348.3 5.0 copy-start.1
  348.3 5.0 copy-start.4
  606.9 1.8 copy-start.3
Sparse Core Ops, SparseCore 0:
  9.8 205.8 all-gather.2
  414.5 111.1 all-gather.4
where the time goes:
time: 619 us; the launch traced here: 617 us
  waiting for transfers between devices  344 us (56%)
  matrix products  107 us (17%)
  local copies, waits for them, and re-layouts  94.3 us (15%)
  blocking collectives  32 us (5%)
  other arithmetic  18 us (3%)
  between operations  13.5 us (2%)
  starting transfers between devices  7.85 us (1%)
    all_gather x1, waiting for transfers between devices, on_device(): whole = lax.all_gather(feats, 'vtx', axis=1, tiled=True)  204 us
    all_gather x1, waiting for transfers between devices, on_device(): whole_two = lax.all_gather(returned, 'vtx', axis=1, tiled=True)  111 us
    gather x32, local copies, waits for them, and re-layouts, row_block(): picked = blocks[ids_here]  92.1 us
    dot_general x16, matrix products, row_block(): jnp.einsum('ktu,kuw->tw', tiles_here, picked, precision=lax.Precision.HIG...  69.3 us
    all_to_all x1, blocking collectives, on_device(): lax.all_to_all(states, 'snap', split_axis=0, concat_axis=1, tiled=True)  32 us
    all_to_all x1, waiting for transfers between devices, on_device(): lax.all_to_all(hidden_one, 'snap', split_axis=1, concat_axis=0, tiled=True)  27.9 us
    dot_general x16, matrix products, advance(): jnp.dot(state_h, w_recur, precision=lax.Precision.HIGHEST)  27.3 us
  transfers between devices with their start and end apart: 3, of which 3 were waited for; matrix products, arithmetic and copies ran while one was open for 1% of the time, Pallas kernels for 0%

commit v1 on v0

--- a/solution.py
+++ b/solution.py
@@ -2,6 +2,27 @@
 import jax.numpy as jnp
 from jax import lax
 from jax.sharding import PartitionSpec as P
+
+
+def collect(x, axis, dim):
+    size, index, extent = (lax.axis_size(axis), lax.axis_index(axis), x.shape[dim])
+    right = [(i, (i + 1) % size) for i in range(size)]
+    behind = [(i, (i - 1) % size) for i in range(size)]
+    result = jnp.zeros((*x.shape[:dim], size * extent, *x.shape[dim + 1 :]), x.dtype)
+    result = lax.dynamic_update_slice_in_dim(result, x, index * extent, axis=dim)
+    from_left = from_right = x
+    half = size // 2
+    for hop in range(1, half + 1):
+        from_left = lax.ppermute(from_left, axis, right)
+        result = lax.dynamic_update_slice_in_dim(
+            result, from_left, (index - hop) % size * extent, axis=dim
+        )
+        if hop < size - half:
+            from_right = lax.ppermute(from_right, axis, behind)
+            result = lax.dynamic_update_slice_in_dim(
+                result, from_right, (index + hop) % size * extent, axis=dim
+            )
+    return result
 
 
 def block_sum(tile_set, column_ids, source):
@@ -53,7 +74,7 @@
     pre_time = jnp.einsum("svh,hg->svg", timelines, w_input, precision=lax.Precision.HIGHEST)
     states = recurrence(pre_time, w_recur, lstm_bias)
     returned = lax.all_to_all(states, "snap", split_axis=0, concat_axis=1, tiled=True)
-    whole_two = lax.all_gather(returned, "vtx", axis=1, tiled=True)
+    whole_two = collect(returned, "vtx", 1)
     mixed_two = scale * (returned + jax.vmap(block_sum)(tiles, col_ids, whole_two))
     return jnp.einsum("svh,hg->svg", mixed_two, w_second, precision=lax.Precision.HIGHEST)
 

time: 619 us -> 734 us (1.19)
  waiting for transfers between devices: 344 us -> 397 us
  starting transfers between devices: 7.85 us -> 41.8 us
  local copies, waits for them, and re-layouts: 94.3 us -> 109 us
  other arithmetic: 18 us -> 28.1 us
    ppermute x0 -> x15, waiting for transfers between devices: none -> 164 us  [the longest x8 164 us: collect(): from_left = lax.ppermute(from_left, axis, right)]
    all_gather x1 -> x0, waiting for transfers between devices: 111 us -> none  [on_device(): whole_two = lax.all_gather(returned, 'vtx', axis=1, tiled=True)]
    ppermute x0 -> x15, starting transfers between devices: none -> 33.9 us  [the longest x7 33 us: collect(): from_right = lax.ppermute(from_right, axis, behind)]
    dynamic_update_slice x16, other arithmetic: 1.36 us -> 11.5 us  [recurrence(): _, states = lax.scan(advance, (zeros, zeros), pre_time)]
    unnamed x11 -> x47, local copies, waits for them, and re-layouts: 0.09 us -> 7.44 us
  transfers between devices with their start and end apart: 3 -> 17, of which waited for: 3 -> 10; matrix products, arithmetic and copies ran while one was open for 1% -> 2% of each run, Pallas kernels for 0% -> 0%
where the time goes in v1:
time: 734 us; the launch traced here: 730 us
  waiting for transfers between devices  397 us (54%)
  local copies, waits for them, and re-layouts  109 us (15%)
  matrix products  108 us (15%)
  starting transfers between devices  41.8 us (6%)
  blocking collectives  32.1 us (4%)
  other arithmetic  28.1 us (4%)
  between operations  13.8 us (2%)
    all_gather x1, waiting for transfers between devices, on_device(): whole = lax.all_gather(feats, 'vtx', axis=1, tiled=True)  204 us
    ppermute x8, waiting for transfers between devices, collect(): from_left = lax.ppermute(from_left, axis, right)  164 us
    gather x32, local copies, waits for them, and re-layouts, row_block(): picked = blocks[ids_here]  92.3 us
    dot_general x16, matrix products, row_block(): jnp.einsum('ktu,kuw->tw', tiles_here, picked, precision=lax.Precision.HIG...  69.4 us
    ppermute x7, starting transfers between devices, collect(): from_right = lax.ppermute(from_right, axis, behind)  33 us
    all_to_all x1, blocking collectives, on_device(): lax.all_to_all(states, 'snap', split_axis=0, concat_axis=1, tiled=True)  32.1 us
    all_to_all x1, waiting for transfers between devices, on_device(): lax.all_to_all(hidden_one, 'snap', split_axis=1, concat_axis=0, tiled=True)  27.9 us
    dot_general x16, matrix products, advance(): jnp.dot(state_h, w_recur, precision=lax.Precision.HIGHEST)  27.3 us
  transfers between devices with their start and end apart: 17, of which 10 were waited for; matrix products, arithmetic and copies ran while one was open for 2% of the time, Pallas kernels for 0%

profile of v1, /device:TPU:1, one launch (start us, length us, event | category | flops | bytes accessed | tf_op | source)
XLA Modules:
  0.0 729.5 jit_solution(17671376433136983278)
XLA Ops:
  11.3 204.4 %all-gather.2.cloned.1.call-done = f32[1,16384,512]{2,1,0:T(8,128)} async-done(((f32[1,1024,512]{2,1,0:T(8,128)}), f32[1,16384,512]{2,1,0:T(8,128)}) %all-gather.2.cloned.1.call-update) | async-done | bytes 33554448 | tf_op jit(solution)/shard_map/all_gather | solution.py:68
  215.7 91.3 %while.35 = (s32[]{:T(128)}, f32[8,1,128,512]{3,2,1,0:T(8,128)}, f32[8,1,16,128,128]{4,3,2,1,0:T(8,128)}, s32[8,1,16]{2,1,0:T(1,128)}, f32[1,128,128,512]{3,2,1,0:T(8,128)}, /*index=5*/s32[]{:T(128)}) while((s32[]{:T(128)}, f32[8,1,128,512]{3,2,1,0:T(8,128)}, f32[8,1,16,128,128]{4,3,2,1,0:T(8,128)}, s32[8,1,16]{2,1,0:T(1,128)}, ...), condition=%wide.region_2.3_spmd, body=%wide.region_1.2_spmd.sunk | while | flops 1610612864 | bytes 13895369 | solution.py:38
  313.3 7.8 %all-to-all-start = ((f32[1,1024,256]{2,0,1:T(1,128)}), f32[1,1024,256]{2,0,1:T(1,128)S(1)}, u32[]{:S(2)}, u32[]{:S(2)}) async-start(f32[1,1024,256]{2,0,1:T(1,128)} %copy.12), calls=%async_computation | async-start | bytes 2097152 | tf_op jit(solution)/shard_map/all_to_all | solution.py:73
  321.1 27.9 %all-to-all-done = f32[1,1024,256]{2,0,1:T(1,128)S(1)} async-done(((f32[1,1024,256]{2,0,1:T(1,128)}), f32[1,1024,256]{2,0,1:T(1,128)S(1)}, u32[]{:S(2)}, u32[]{:S(2)}) %all-to-all-start) | async-done | bytes 1048608 | tf_op jit(solution)/shard_map/all_to_all | solution.py:73
  354.2 38.8 %while.37 = (s32[]{:T(128)}, f32[64,256]{1,0:T(8,128)S(1)}, f32[64,256]{1,0:T(8,128)S(1)}, f32[16,64,256]{2,1,0:T(8,128)}, f32[16,64,1024]{2,1,0:T(8,128)}, /*in...) while((s32[]{:T(128)}, f32[64,256]{1,0:T(8,128)S(1)}, ...), condition=%wide.region_4.5_spmd.clone, body=%wide.region_3.4_spmd.clone.sunk | while | flops 201703424 | bytes 2167404 | solution.py:62
  393.0 32.1 %all_to_all.27 = f32[16,64,256]{2,1,0:T(8,128)S(1)} all-to-all(f32[16,64,256]{2,1,0:T(8,128)} %get-tuple-element.97), channel_id=1, replica_groups=mesh['snap'=16,'vtx'=16] {'snap'}, dimensions={0} | all-to-all | bytes 2097152 | tf_op jit(solution)/shard_map/all_to_all | solution.py:76
  429.9 22.7 %collective-permute-done = f32[1,1024,256]{2,1,0:T(8,128)S(1)} collective-permute-done((f32[1,1024,256]{2,1,0:T(8,128)S(1)}, f32[1,1024,256]{2,1,0:T(8,128)S(1)}, u32[]{:S(2)}, u32[]{:S(2)}) %collective-permute-start) | collective-permute-done | bytes 1048608 | tf_op jit(solution)/shard_map/ppermute | solution.py:16
  457.6 23.1 %collective-permute-done.2 = f32[1,1024,256]{2,1,0:T(8,128)S(1)} collective-permute-done((f32[1,1024,256]{2,1,0:T(8,128)S(1)}, f32[1,1024,256]{2,1,0:T(8,128)S(1)}, u32[]{:S(2)}, u32[]{:S(2)}) %collective-permute-start.2) | collective-permute-done | bytes 1048608 | tf_op jit(solution)/shard_map/ppermute | solution.py:16
  485.5 22.4 %collective-permute-done.4 = f32[1,1024,256]{2,1,0:T(8,128)S(1)} collective-permute-done((f32[1,1024,256]{2,1,0:T(8,128)S(1)}, f32[1,1024,256]{2,1,0:T(8,128)S(1)}, u32[]{:S(2)}, u32[]{:S(2)}) %collective-permute-start.4) | collective-permute-done | bytes 1048608 | tf_op jit(solution)/shard_map/ppermute | solution.py:16
  512.8 21.4 %collective-permute-done.6 = f32[1,1024,256]{2,1,0:T(8,128)S(1)} collective-permute-done((f32[1,1024,256]{2,1,0:T(8,128)S(1)}, f32[1,1024,256]{2,1,0:T(8,128)S(1)}, u32[]{:S(2)}, u32[]{:S(2)}) %collective-permute-start.6) | collective-permute-done | bytes 1048608 | tf_op jit(solution)/shard_map/ppermute | solution.py:16
  540.0 20.6 %collective-permute-done.8 = f32[1,1024,256]{2,1,0:T(8,128)S(1)} collective-permute-done((f32[1,1024,256]{2,1,0:T(8,128)S(1)}, f32[1,1024,256]{2,1,0:T(8,128)S(1)}, u32[]{:S(2)}, u32[]{:S(2)}) %collective-permute-start.8) | collective-permute-done | bytes 1048608 | tf_op jit(solution)/shard_map/ppermute | solution.py:16
  565.5 19.7 %collective-permute-done.10 = f32[1,1024,256]{2,1,0:T(8,128)} collective-permute-done((f32[1,1024,256]{2,1,0:T(8,128)S(1)}, f32[1,1024,256]{2,1,0:T(8,128)}, u32[]{:S(2)}, u32[]{:S(2)}) %collective-permute-start.10) | collective-permute-done | bytes 1048608 | tf_op jit(solution)/shard_map/ppermute | solution.py:16
  592.4 16.7 %collective-permute-done.12 = f32[1,1024,256]{2,1,0:T(8,128)} collective-permute-done((f32[1,1024,256]{2,1,0:T(8,128)}, f32[1,1024,256]{2,1,0:T(8,128)}, u32[]{:S(2)}, u32[]{:S(2)}) %collective-permute-start.12) | collective-permute-done | bytes 1048608 | tf_op jit(solution)/shard_map/ppermute | solution.py:16
  614.6 17.2 %collective-permute-done.14 = f32[1,1024,256]{2,1,0:T(8,128)S(1)} collective-permute-done((f32[1,1024,256]{2,1,0:T(8,128)}, f32[1,1024,256]{2,1,0:T(8,128)S(1)}, u32[]{:S(2)}, u32[]{:S(2)}) %collective-permute-start.14) | collective-permute-done | bytes 1048608 | tf_op jit(solution)/shard_map/ppermute | solution.py:16
  632.0 5.8 copy-done.1
  637.7 81.2 %while.36 = (s32[]{:T(128)}, f32[8,1,128,256]{3,2,1,0:T(8,128)}, f32[8,1,16,128,128]{4,3,2,1,0:T(8,128)}, s32[8,1,16]{2,1,0:T(1,128)}, f32[1,128,128,256]{3,2,1,0:T(8,128)}, /*index=5*/s32[]{:T(128)}) while((s32[]{:T(128)}, f32[8,1,128,256]{3,2,1,0:T(8,128)}, f32[8,1,16,128,128]{4,3,2,1,0:T(8,128)}, s32[8,1,16]{2,1,0:T(1,128)}, ...), condition=%wide.region_6.7_spmd, body=%wide.region_5.6_spmd.sunk | while | flops 805306496 | bytes 7472841 | solution.py:38
  638.4 6.4 gather_fusion.1
  648.6 6.4 gather_fusion.1
  658.7 6.4 gather_fusion.1
  668.9 6.4 gather_fusion.1
  679.0 6.4 gather_fusion.1
  689.2 6.4 gather_fusion.1
  699.3 6.4 gather_fusion.1
  709.5 6.4 gather_fusion.1
  (203 shorter events, 222.2 us)
Async XLA Ops:
  6.5 342.6 %copy-start = (f32[256,1024]{1,0:T(8,128)S(1)}, f32[256,1024]{1,0:T(8,128)}, u32[]{:S(2)}) copy-start(f32[256,1024]{1,0:T(8,128)} %param.18) | copy-start | bytes 3145732
  6.5 209.2 %all-gather.2.cloned.1.call-start = ((), (), s32[]{:S(2)}) async-start(), calls=%async_computation.2 | async-start | bytes 35651584 | tf_op jit(solution)/shard_map/all_gather | solution.py:68
  215.7 91.3 %copy-start.20 = (f32[512,256]{1,0:T(8,128)S(1)}, f32[512,256]{1,0:T(8,128)}, u32[]{:S(2)}) copy-start(f32[512,256]{1,0:T(8,128)} %param.17) | copy-start | bytes 1572868
  307.0 47.2 %copy-start.22 = (f32[1024]{0:T(1024)S(1)}, f32[1024]{0:T(1024)}, u32[]{:S(2)}) copy-start(f32[1024]{0:T(1024)} %param.20) | copy-start | bytes 12292
  313.3 35.8 %all-to-all-start = ((f32[1,1024,256]{2,0,1:T(1,128)}), f32[1,1024,256]{2,0,1:T(1,128)S(1)}, u32[]{:S(2)}, u32[]{:S(2)}) async-start(f32[1,1024,256]{2,0,1:T(1,128)} %copy.12), calls=%async_computation | async-start | bytes 2097152 | tf_op jit(solution)/shard_map/all_to_all | solution.py:73
  425.1 184.0 %copy-start.3 = (f32[16,64,256]{2,1,0:T(8,128)}, f32[16,64,256]{2,1,0:T(8,128)S(1)}, u32[]{:S(2)}) copy-start(f32[16,64,256]{2,1,0:T(8,128)S(1)} %all_to_all.27) | copy-start | bytes 3145732
  425.1 27.5 %collective-permute-start = (f32[1,1024,256]{2,1,0:T(8,128)S(1)}, f32[1,1024,256]{2,1,0:T(8,128)S(1)}, u32[]{:S(2)}, u32[]{:S(2)}) collective-permute-start(f32[1,1024,256]{2,1,0:T(8,128)S(1)} %bitcast.112), channel_id=1, source_target_pairs={{0,1},{1,2},{2,3},{3,4},{4,5},{5,6},{6,7},{7,8},{8,9},{9,10},{10,1... | collective-permute-start | bytes 3145736 | tf_op jit(solution)/shard_map/ppermute | solution.py:16
  426.0 26.5 %collective-permute-start.1 = (f32[1,1024,256]{2,1,0:T(8,128)S(1)}, f32[1,1024,256]{2,1,0:T(8,128)S(1)}, u32[]{:S(2)}, u32[]{:S(2)}) collective-permute-start(f32[1,1024,256]{2,1,0:T(8,128)S(1)} %bitcast.113), channel_id=1, source_target_pairs={{0,15},{1,0},{2,1},{3,2},{4,3},{5,4},{6,5},{7,6},{8,7},{9,8},{10,9... | collective-permute-start | bytes 3145736 | tf_op jit(solution)/shard_map/ppermute | solution.py:21
  452.5 28.1 %collective-permute-start.2 = (f32[1,1024,256]{2,1,0:T(8,128)S(1)}, f32[1,1024,256]{2,1,0:T(8,128)S(1)}, u32[]{:S(2)}, u32[]{:S(2)}) collective-permute-start(f32[1,1024,256]{2,1,0:T(8,128)S(1)} %collective-permute-done), channel_id=1, source_target_pairs={{0,1},{1,2},{2,3},{3,4},{4,5},{5,6},{6,7},{7,8},{8,9},{9,10},{10,1... | collective-permute-start | bytes 3145736 | tf_op jit(solution)/shard_map/ppermute | solution.py:16
  452.6 28.1 %collective-permute-start.3 = (f32[1,1024,256]{2,1,0:T(8,128)S(1)}, f32[1,1024,256]{2,1,0:T(8,128)S(1)}, u32[]{:S(2)}, u32[]{:S(2)}) collective-permute-start(f32[1,1024,256]{2,1,0:T(8,128)S(1)} %collective-permute-done.1), channel_id=1, source_target_pairs={{0,15},{1,0},{2,1},{3,2},{4,3},{5,4},{6,5},{7,6},{8,7},{9,8},{10,9... | collective-permute-start | bytes 3145736 | tf_op jit(solution)/shard_map/ppermute | solution.py:21
  480.7 79.9 %copy-start.8 = (f32[1,1024,256]{2,1,0:T(8,128)}, f32[1,1024,256]{2,1,0:T(8,128)S(1)}, u32[]{:S(2)}) copy-start(f32[1,1024,256]{2,1,0:T(8,128)S(1)} %collective-permute-done.2) | copy-start | bytes 3145732
  480.7 27.2 %collective-permute-start.4 = (f32[1,1024,256]{2,1,0:T(8,128)S(1)}, f32[1,1024,256]{2,1,0:T(8,128)S(1)}, u32[]{:S(2)}, u32[]{:S(2)}) collective-permute-start(f32[1,1024,256]{2,1,0:T(8,128)S(1)} %collective-permute-done.2), channel_id=1, source_target_pairs={{0,1},{1,2},{2,3},{3,4},{4,5},{5,6},{6,7},{7,8},{8,9},{9,10},{10,1... | collective-permute-start | bytes 3145736 | tf_op jit(solution)/shard_map/ppermute | solution.py:16
  480.7 27.2 %collective-permute-start.5 = (f32[1,1024,256]{2,1,0:T(8,128)S(1)}, f32[1,1024,256]{2,1,0:T(8,128)S(1)}, u32[]{:S(2)}, u32[]{:S(2)}) collective-permute-start(f32[1,1024,256]{2,1,0:T(8,128)S(1)} %collective-permute-done.3), channel_id=1, source_target_pairs={{0,15},{1,0},{2,1},{3,2},{4,3},{5,4},{6,5},{7,6},{8,7},{9,8},{10,9... | collective-permute-start | bytes 3145736 | tf_op jit(solution)/shard_map/ppermute | solution.py:21
  507.9 26.3 %collective-permute-start.6 = (f32[1,1024,256]{2,1,0:T(8,128)S(1)}, f32[1,1024,256]{2,1,0:T(8,128)S(1)}, u32[]{:S(2)}, u32[]{:S(2)}) collective-permute-start(f32[1,1024,256]{2,1,0:T(8,128)S(1)} %collective-permute-done.4), channel_id=1, source_target_pairs={{0,1},{1,2},{2,3},{3,4},{4,5},{5,6},{6,7},{7,8},{8,9},{9,10},{10,1... | collective-permute-start | bytes 3145736 | tf_op jit(solution)/shard_map/ppermute | solution.py:16
  507.9 52.7 %copy-start.12 = (f32[1,1024,256]{2,1,0:T(8,128)}, f32[1,1024,256]{2,1,0:T(8,128)S(1)}, u32[]{:S(2)}) copy-start(f32[1,1024,256]{2,1,0:T(8,128)S(1)} %collective-permute-done.5) | copy-start | bytes 3145732
  507.9 27.3 %collective-permute-start.7 = (f32[1,1024,256]{2,1,0:T(8,128)S(1)}, f32[1,1024,256]{2,1,0:T(8,128)S(1)}, u32[]{:S(2)}, u32[]{:S(2)}) collective-permute-start(f32[1,1024,256]{2,1,0:T(8,128)S(1)} %collective-permute-done.5), channel_id=1, source_target_pairs={{0,15},{1,0},{2,1},{3,2},{4,3},{5,4},{6,5},{7,6},{8,7},{9,8},{10,9... | collective-permute-start | bytes 3145736 | tf_op jit(solution)/shard_map/ppermute | solution.py:21
  535.2 25.4 %collective-permute-start.8 = (f32[1,1024,256]{2,1,0:T(8,128)S(1)}, f32[1,1024,256]{2,1,0:T(8,128)S(1)}, u32[]{:S(2)}, u32[]{:S(2)}) collective-permute-start(f32[1,1024,256]{2,1,0:T(8,128)S(1)} %collective-permute-done.6), channel_id=1, source_target_pairs={{0,1},{1,2},{2,3},{3,4},{4,5},{5,6},{6,7},{7,8},{8,9},{9,10},{10,1... | collective-permute-start | bytes 3145736 | tf_op jit(solution)/shard_map/ppermute | solution.py:16
  535.2 25.4 %collective-permute-start.9 = (f32[1,1024,256]{2,1,0:T(8,128)S(1)}, f32[1,1024,256]{2,1,0:T(8,128)}, u32[]{:S(2)}, u32[]{:S(2)}) collective-permute-start(f32[1,1024,256]{2,1,0:T(8,128)S(1)} %collective-permute-done.7), channel_id=1, source_target_pairs={{0,15},{1,0},{2,1},{3,2},{4,3},{5,4},{6,5},{7,6},{8,7},{9,8},{10,9... | collective-permute-start | bytes 3145736 | tf_op jit(solution)/shard_map/ppermute | solution.py:21
  560.6 24.6 %collective-permute-start.10 = (f32[1,1024,256]{2,1,0:T(8,128)S(1)}, f32[1,1024,256]{2,1,0:T(8,128)}, u32[]{:S(2)}, u32[]{:S(2)}) collective-permute-start(f32[1,1024,256]{2,1,0:T(8,128)S(1)} %collective-permute-done.8), channel_id=1, source_target_pairs={{0,1},{1,2},{2,3},{3,4},{4,5},{5,6},{6,7},{7,8},{8,9},{9,10},{10,1... | collective-permute-start | bytes 3145736 | tf_op jit(solution)/shard_map/ppermute | solution.py:16
  560.6 26.8 %collective-permute-start.11 = (f32[1,1024,256]{2,1,0:T(8,128)}, f32[1,1024,256]{2,1,0:T(8,128)}, u32[]{:S(2)}, u32[]{:S(2)}) collective-permute-start(f32[1,1024,256]{2,1,0:T(8,128)} %collective-permute-done.9), channel_id=1, source_target_pairs={{0,15},{1,0},{2,1},{3,2},{4,3},{5,4},{6,5},{7,6},{8,7},{9,8},{10,9... | collective-permute-start | bytes 3145736 | tf_op jit(solution)/shard_map/ppermute | solution.py:21
  585.2 23.9 %collective-permute-start.12 = (f32[1,1024,256]{2,1,0:T(8,128)}, f32[1,1024,256]{2,1,0:T(8,128)}, u32[]{:S(2)}, u32[]{:S(2)}) collective-permute-start(f32[1,1024,256]{2,1,0:T(8,128)} %collective-permute-done.10), channel_id=1, source_target_pairs={{0,1},{1,2},{2,3},{3,4},{4,5},{5,6},{6,7},{7,8},{8,9},{9,10},{10,1... | collective-permute-start | bytes 3145736 | tf_op jit(solution)/shard_map/ppermute | solution.py:16
  587.4 27.1 %collective-permute-start.13 = (f32[1,1024,256]{2,1,0:T(8,128)}, f32[1,1024,256]{2,1,0:T(8,128)S(1)}, u32[]{:S(2)}, u32[]{:S(2)}) collective-permute-start(f32[1,1024,256]{2,1,0:T(8,128)} %collective-permute-done.11), channel_id=1, source_target_pairs={{0,15},{1,0},{2,1},{3,2},{4,3},{5,4},{6,5},{7,6},{8,7},{9,8},{10,9... | collective-permute-start | bytes 3145736 | tf_op jit(solution)/shard_map/ppermute | solution.py:21
  609.0 22.8 %collective-permute-start.14 = (f32[1,1024,256]{2,1,0:T(8,128)}, f32[1,1024,256]{2,1,0:T(8,128)S(1)}, u32[]{:S(2)}, u32[]{:S(2)}) collective-permute-start(f32[1,1024,256]{2,1,0:T(8,128)} %collective-permute-done.12), channel_id=1, source_target_pairs={{0,1},{1,2},{2,3},{3,4},{4,5},{5,6},{6,7},{7,8},{8,9},{9,10},{10,1... | collective-permute-start | bytes 3145736 | tf_op jit(solution)/shard_map/ppermute | solution.py:16
  637.7 83.0 %copy-start.21 = (f32[256,256]{1,0:T(8,128)S(1)}, f32[256,256]{1,0:T(8,128)}, u32[]{:S(2)}) copy-start(f32[256,256]{1,0:T(8,128)} %param.21) | copy-start | bytes 786436
  (16 other events, 230.1 us)
Sparse Core Ops, SparseCore 0:
  9.8 205.8 all-gather.1
